TPU v7x, 512 devices: a whole 4x8x8 slice. The times are simulated.
512 devices in a mesh: prow: 32 (over x, z), pcol: 16 (over y, core).
Axes of the slice: x: 4, y: 8, z: 8, core: 2. Of those that a mesh axis runs over, the one named last changes fastest.
Arguments:
- inverse_block: float32 [4, 32, 128, 8, 16, 128], P(None, 'prow', None, None, 'pcol'), may hold values from -6 to 6
- panel_first: float32 [4, 32, 256, 128], P(None, 'prow', 'pcol'), may hold values from -0.046875 to 0.046875
- panel_second: float32 [4, 32, 256, 128], P(None, 'prow', 'pcol'), may hold values from -0.046875 to 0.046875
- coupling: float32 [256, 256], P('prow'), may hold values from -0.375 to 0.375
- dinv_first: float32 [256, 256], replicated, may hold values from -6 to 6
- dinv_second: float32 [256, 256], replicated, may hold values from -6 to 6
- struct_first: int32 [128], replicated, may hold values 0 or 1
- struct_second: int32 [128], replicated, may hold values 0 or 1
Outputs:
- row_first: float32 [8, 16, 256, 128], P(None, 'pcol', 'prow')
- own_first: float32 [256, 256], replicated
- row_second: float32 [8, 16, 256, 128], P(None, 'pcol', 'prow')
- cross: float32 [256, 256], replicated
- own_second: float32 [256, 256], replicated
Inputs may be any that keep to these rules, and one draw needn't show every extreme that they name: `struct_first`: 1 marks a block that lies in the supernode's structure, 0 one that does not. `struct_second`: 1 marks a block that lies in the supernode's structure, 0 one that does not.
All inputs are finite; a program needn't handle non-finite values.
Results may differ from a plain program's by a relative error of at most 0.000084.
Values sent between devices are 32-bit elements; how exact they have to be, the bound alone decides.
A program may use at most 64 MiB of HBM per device.

v0:
```python
import jax
import jax.numpy as jnp
from jax import lax
from jax.sharding import PartitionSpec as P


def body(
    inverse_block,
    panel_first,
    panel_second,
    coupling,
    dinv_first,
    dinv_second,
    struct_first,
    struct_second,
):
    highest = lax.Precision.HIGHEST
    rows = lax.axis_size("prow")
    cols = lax.axis_size("pcol")
    prow_index = lax.axis_index("prow")
    pcol_index = lax.axis_index("pcol")
    ratio = rows // cols
    row_blocks = inverse_block.shape[0]
    blk = inverse_block.shape[2]
    col_blocks = inverse_block.shape[3]
    slab = coupling.shape[0]
    width = coupling.shape[1]
    local = inverse_block.reshape(row_blocks, blk, col_blocks, blk)
    diagonal = (prow_index % cols == pcol_index).astype(jnp.float32)

    def row_mask(struct):
        table = struct.astype(jnp.float32).reshape(row_blocks, rows)
        return lax.dynamic_slice_in_dim(table, prow_index, 1, 1)[:, :, None]

    def col_mask(struct):
        table = struct.astype(jnp.float32).reshape(col_blocks, cols)
        return lax.dynamic_slice_in_dim(table, pcol_index, 1, 1)[:, :, None]

    def matching(full):
        grouped = full.reshape(row_blocks, ratio, width, blk)
        return lax.dynamic_slice_in_dim(grouped, prow_index // cols, 1, 1)[:, 0]

    def my_rows(full):
        return lax.dynamic_slice_in_dim(full, prow_index * slab, slab, 1)

    def product(panel, mask):
        return jnp.einsum("rwx,rxcy->cwy", panel * mask, local, precision=highest)

    panel_a = lax.all_gather(panel_first, "pcol", axis=2, tiled=True)[:, 0]
    panel_b = lax.all_gather(panel_second, "pcol", axis=2, tiled=True)[:, 0]
    coupling_full = lax.all_gather(coupling, "prow", axis=0, tiled=True)
    rmask_a = row_mask(struct_first)
    rmask_b = row_mask(struct_second)
    cmask_a = col_mask(struct_first)
    cmask_b = col_mask(struct_second)
    part_a = product(panel_a, rmask_a)
    part_b = product(panel_b, rmask_b)
    row_a = -lax.psum(part_a, "prow") * cmask_a
    carried = jnp.einsum("av,cay->cvy", coupling, my_rows(row_a), precision=highest)
    row_b = -lax.psum(part_b + carried, "prow") * cmask_b
    chosen_a = matching(row_a)
    chosen_b = matching(row_b)
    mine_a = my_rows(row_a)
    mine_b = my_rows(row_b)
    term_a = jnp.einsum("rwy,rvy->wv", chosen_a, panel_a, precision=highest) * diagonal
    column_a = lax.psum(term_a, "prow")
    own_a = dinv_first - lax.psum(column_a, "pcol")
    own_rows = lax.dynamic_slice_in_dim(own_a, prow_index * slab, slab, 0)
    cross_term = (
        jnp.einsum("rvy,ray->va", panel_b * rmask_b, chosen_a, precision=highest)
        + jnp.einsum("av,aw->vw", coupling, own_rows, precision=highest)
    ) * diagonal
    own_term = jnp.einsum("rvy,ruy->vu", chosen_b, panel_b, precision=highest) * diagonal
    cross_col, own_col = lax.psum((cross_term, own_term), "prow")
    cross_sum, own_sum = lax.psum((cross_col, own_col), "pcol")
    cross = -cross_sum
    own_b = dinv_second - own_sum - jnp.dot(cross, coupling_full, precision=highest)
    out_a = mine_a.reshape(col_blocks, 1, slab, blk)
    out_b = mine_b.reshape(col_blocks, 1, slab, blk)
    return (out_a, own_a, out_b, cross, own_b)


def solution(mesh):
    return jax.shard_map(
        body,
        mesh=mesh,
        in_specs=(
            P(None, "prow", None, None, "pcol", None),
            P(None, "prow", "pcol", None),
            P(None, "prow", "pcol", None),
            P("prow", None),
            P(),
            P(),
            P(),
            P(),
        ),
        out_specs=(P(None, "pcol", "prow", None), P(), P(None, "pcol", "prow", None), P(), P()),
        check_vma=False,
    )
```

profile of v0, /device:TPU:1, one launch (start us, length us, event | category | flops | bytes accessed | tf_op | source)
XLA Modules:
  0.0 760.0 jit_solution(10065821596533365772)
XLA Ops:
  7.2 0.8 convert_element_type.11
  8.1 22.7 %all_gather.9 = f32[4,1,256,128]{3,2,0,1:T(8,128)S(1)} all-gather(f32[4,1,16,128]{3,2,0,1:T(8,128)} %bitcast.74), channel_id=1, replica_groups=mesh['prow'=32,'pcol'=16] {'pcol'}, dimensions={2}, use_global_device_ids=true | all-gather | bytes 557056 | tf_op jit(solution)/shard_map/all_gather | solution.py:49
  31.0 3.1 fusion.4
  34.8 17.4 %all_gather.10 = f32[4,1,256,128]{3,2,0,1:T(8,128)S(1)} all-gather(f32[4,1,16,128]{3,2,0,1:T(8,128)S(1)} %bitcast.75), channel_id=1, replica_groups=mesh['prow'=32,'pcol'=16] {'pcol'}, dimensions={2}, use_global_device_ids=true | all-gather | bytes 557056 | tf_op jit(solution)/shard_map/all_gather | solution.py:50
  52.1 3.1 fusion.7
  55.3 134.7 %all-reduce.9.cloned.1.call-done = f32[8,256,128]{2,1,0:T(8,128)} async-done(((f32[8,256,128]{2,1,0:T(8,128)}), f32[8,256,128]{2,1,0:T(8,128)}) %all-reduce.9.cloned.1.call-update) | async-done | bytes 1048592 | tf_op jit(solution)/shard_map/psum | solution.py:58
  190.0 1.4 negate_multiply_fusion.1
  191.5 1.3 fusion.12
  192.8 2.0 fusion.10
  195.1 1.7 convolution_bitcast_fusion.2
  196.8 157.6 %all-reduce.15.cloned.1.call-done = (f32[256,256]{1,0:T(8,128)}, f32[8,256,128]{2,1,0:T(8,128)}) async-done(((f32[256,256]{1,0:T(8,128)}, f32[8,256,128]{2,1,0:T(8,128)}), (f32[256,256]{1,0:T(8,128)}, f32[8,256,128]{2,1,0:T(8,128)})) %all-reduce.15.cloned.1.call-update) | async-done | bytes 1310736 | tf_op jit(solution)/shard_map/psum | solution.py:66
  354.5 1.4 negate_multiply_fusion
  355.9 1.0 copy-done.3
  356.9 1.3 fusion.11
  358.2 113.8 %all-reduce.11.cloned.1.call-done = f32[256,256]{1,0:T(8,128)} async-done(((f32[256,256]{1,0:T(8,128)}), f32[256,256]{1,0:T(8,128)}) %all-reduce.11.cloned.1.call-update) | async-done | bytes 262160 | tf_op jit(solution)/shard_map/psum | solution.py:67
  472.1 1.0 sub.15
  473.1 1.1 fusion.14
  474.3 157.2 %all-reduce.13.cloned.1.call-done = (f32[256,256]{1,0:T(8,128)}, f32[256,256]{1,0:T(8,128)}) async-done(((f32[256,256]{1,0:T(8,128)}, f32[256,256]{1,0:T(8,128)}), (f32[256,256]{1,0:T(8,128)}, f32[256,256]{1,0:T(8,128)})) %all-reduce.13.cloned.1.call-update) | async-done | bytes 524304 | tf_op jit(solution)/shard_map/psum | solution.py:74
  631.5 35.0 %all_gather.11 = f32[256,256]{1,0:T(8,128)S(1)} all-gather(f32[8,256]{1,0:T(8,128)S(1)} %copy-done.8), channel_id=1, replica_groups=mesh['prow'=32,'pcol'=16] {'prow'}, dimensions={0}, use_global_device_ids=true | all-gather | bytes 270336 | tf_op jit(solution)/shard_map/all_gather | solution.py:51
  666.6 1.4 dynamic-slice_bitcast_fusion.1
  668.0 1.4 dynamic-slice_bitcast_fusion
  669.3 81.0 %all-reduce.17.cloned.1.call-done = (f32[256,256]{1,0:T(8,128)}, f32[256,256]{1,0:T(8,128)}) async-done(((f32[256,256]{1,0:T(8,128)}, f32[256,256]{1,0:T(8,128)}), (f32[256,256]{1,0:T(8,128)}, f32[256,256]{1,0:T(8,128)})) %all-reduce.17.cloned.1.call-update) | async-done | bytes 524304 | tf_op jit(solution)/shard_map/psum | solution.py:75
  750.3 1.0 neg.11
  751.3 2.1 convolution_subtract_fusion
  (40 shorter events, 1.4 us)
Async XLA Ops:
  7.2 23.8 %copy-start = (f32[4,1,128,8,1,128]{5,4,3,2,1,0:T(1,128)S(1)}, f32[4,1,128,8,1,128]{5,4,3,2,1,0:T(1,128)}, u32[]{:S(2)}) copy-start(f32[4,1,128,8,1,128]{5,4,3,2,1,0:T(1,128)} %param.8) | copy-start | bytes 6291460
  7.2 182.8 %all-reduce.9.cloned.1.call-start = ((), (), s32[]{:S(2)}) async-start(), calls=%async_computation | async-start | bytes 2097152 | tf_op jit(solution)/shard_map/psum | solution.py:58
  31.0 3.3 copy-start.10
  31.0 3.8 copy-start.9
  34.1 320.3 %all-reduce.15.cloned.1.call-start = ((), (), s32[]{:S(2)}) async-start(), calls=%async_computation.3 | async-start | bytes 2621440 | tf_op jit(solution)/shard_map/psum | solution.py:66
  55.3 137.5 %copy-start.8 = (f32[8,256]{1,0:T(8,128)S(1)}, f32[8,256]{1,0:T(8,128)}, u32[]{:S(2)}) copy-start(f32[8,256]{1,0:T(8,128)} %param.11) | copy-start | bytes 24580
  190.0 2.8 copy-start.2
  191.4 1.3 copy-start.1
  194.8 277.2 %all-reduce.11.cloned.1.call-start = ((), (), s32[]{:S(2)}) async-start(), calls=%async_computation.1 | async-start | bytes 524288 | tf_op jit(solution)/shard_map/psum | solution.py:67
  196.8 275.3 %copy-start.6 = (f32[256,256]{1,0:T(8,128)S(1)}, f32[256,256]{1,0:T(8,128)}, u32[]{:S(2)}) copy-start(f32[256,256]{1,0:T(8,128)} %param.12) | copy-start | bytes 786436
  354.5 277.0 %all-reduce.13.cloned.1.call-start = ((), (), s32[]{:S(2)}) async-start(), calls=%async_computation.2 | async-start | bytes 1048576 | tf_op jit(solution)/shard_map/psum | solution.py:74
  355.9 1.0 copy-start.3
  358.2 393.1 %copy-start.7 = (f32[256,256]{1,0:T(8,128)S(1)}, f32[256,256]{1,0:T(8,128)}, u32[]{:S(2)}) copy-start(f32[256,256]{1,0:T(8,128)} %param.13) | copy-start | bytes 786436
  473.1 280.4 %copy-start.5 = (f32[256,256]{1,0:T(8,128)}, f32[256,256]{1,0:T(8,128)S(1)}, u32[]{:S(2)}) copy-start(f32[256,256]{1,0:T(8,128)S(1)} %sub.15) | copy-start | bytes 786436
  474.2 276.0 %all-reduce.17.cloned.1.call-start = ((), (), s32[]{:S(2)}) async-start(), calls=%async_computation.4 | async-start | bytes 1048576 | tf_op jit(solution)/shard_map/psum | solution.py:75
  751.3 2.2 copy-start.4
Sparse Core Ops, SparseCore 0:
  34.3 155.6 all-reduce.8
  195.0 159.4 all-reduce.14
  356.9 115.1 all-reduce.10
  475.9 155.5 all-reduce.12
  633.9 116.3 all-reduce.16
where the time goes:
time: 760 us
  waiting for transfers between devices  644 us (85%)
  blocking collectives  75.1 us (10%)
  matrix products  15.9 us (2%)
  between operations  13.9 us (2%)
    psum x1, waiting for transfers between devices, body(): column_a = lax.psum(term_a, 'prow')  158 us
    psum x1, waiting for transfers between devices, body(): cross_col, own_col = lax.psum((cross_term, own_term), 'prow')  157 us
    psum x1, waiting for transfers between devices, body(): row_a = -lax.psum(part_a, 'prow') * cmask_a  135 us
    psum x1, waiting for transfers between devices, body(): own_a = dinv_first - lax.psum(column_a, 'pcol')  114 us
    psum x1, waiting for transfers between devices, body(): cross_sum, own_sum = lax.psum((cross_col, own_col), 'pcol')  81 us
    all_gather x1, blocking collectives, body(): coupling_full = lax.all_gather(coupling, 'prow', axis=0, tiled=True)  35 us
    all_gather x1, blocking collectives, body(): panel_a = lax.all_gather(panel_first, 'pcol', axis=2, tiled=True)[:, 0]  22.7 us
    all_gather x1, blocking collectives, body(): panel_b = lax.all_gather(panel_second, 'pcol', axis=2, tiled=True)[:, 0]  17.4 us
  transfers between devices with their start and end apart: 5, of which 5 were waited for; matrix products, arithmetic and copies ran while one was open for 1% of the time, Pallas kernels for 0%

commit v1 on v0

--- a/solution.py
+++ b/solution.py
@@ -63,7 +63,7 @@
     mine_a = my_rows(row_a)
     mine_b = my_rows(row_b)
     term_a = jnp.einsum("rwy,rvy->wv", chosen_a, panel_a, precision=highest) * diagonal
-    column_a = lax.psum(term_a, "prow")
+    column_a = jnp.sum(lax.all_gather(term_a, "prow"), axis=0)
     own_a = dinv_first - lax.psum(column_a, "pcol")
     own_rows = lax.dynamic_slice_in_dim(own_a, prow_index * slab, slab, 0)
     cross_term = (

time: 760 us -> 867 us (1.14)
  waiting for transfers between devices: 644 us -> 742 us
    all_gather x0 -> x1, waiting for transfers between devices: none -> 107 us  [body(): column_a = jnp.sum(lax.all_gather(term_a, 'prow'), axis=0)]
  transfers between devices with their start and end apart: 5 -> 6, of which waited for: 5 -> 6; matrix products, arithmetic and copies ran while one was open for 1% -> 2% of each run, Pallas kernels for 0% -> 0%
where the time goes in v1:
time: 867 us; the launch traced here: 866 us
  waiting for transfers between devices  742 us (86%)
  blocking collectives  75.3 us (9%)
  matrix products  17.9 us (2%)
  between operations  14.2 us (2%)
  other arithmetic  11.1 us (1%)
    psum x1, waiting for transfers between devices, body(): cross_col, own_col = lax.psum((cross_term, own_term), 'prow')  158 us
    psum x1, waiting for transfers between devices, body(): row_b = -lax.psum(part_b + carried, 'prow') * cmask_b  154 us
    psum x1, waiting for transfers between devices, body(): row_a = -lax.psum(part_a, 'prow') * cmask_a  135 us
    psum x1, waiting for transfers between devices, body(): own_a = dinv_first - lax.psum(column_a, 'pcol')  108 us
    all_gather x1, waiting for transfers between devices, body(): column_a = jnp.sum(lax.all_gather(term_a, 'prow'), axis=0)  107 us
    psum x1, waiting for transfers between devices, body(): cross_sum, own_sum = lax.psum((cross_col, own_col), 'pcol')  80.7 us
    all_gather x1, blocking collectives, body(): coupling_full = lax.all_gather(coupling, 'prow', axis=0, tiled=True)  35.1 us
    all_gather x1, blocking collectives, body(): panel_a = lax.all_gather(panel_first, 'pcol', axis=2, tiled=True)[:, 0]  22.8 us
  transfers between devices with their start and end apart: 6, of which 6 were waited for; matrix products, arithmetic and copies ran while one was open for 2% of the time, Pallas kernels for 0%

profile of v1, /device:TPU:1, one launch (start us, length us, event | category | flops | bytes accessed | tf_op | source)
XLA Modules:
  0.0 866.1 jit_solution(9964754084088746575)
XLA Ops:
  7.2 22.8 %all_gather.15 = f32[4,1,256,128]{3,2,0,1:T(8,128)S(1)} all-gather(f32[4,1,16,128]{3,2,0,1:T(8,128)} %bitcast.76), channel_id=1, replica_groups=mesh['prow'=32,'pcol'=16] {'pcol'}, dimensions={2}, use_global_device_ids=true | all-gather | bytes 557056 | tf_op jit(solution)/shard_map/all_gather | solution.py:49
  31.0 3.1 fusion.4
  34.8 17.4 %all_gather.18 = f32[4,1,256,128]{3,2,0,1:T(8,128)S(1)} all-gather(f32[4,1,16,128]{3,2,0,1:T(8,128)S(1)} %bitcast.77), channel_id=1, replica_groups=mesh['prow'=32,'pcol'=16] {'pcol'}, dimensions={2}, use_global_device_ids=true | all-gather | bytes 557056 | tf_op jit(solution)/shard_map/all_gather | solution.py:50
  52.1 3.1 fusion.7
  55.2 134.8 %all-reduce.8.cloned.1.call-done = f32[8,256,128]{2,1,0:T(8,128)} async-done(((f32[8,256,128]{2,1,0:T(8,128)}), f32[8,256,128]{2,1,0:T(8,128)}) %all-reduce.8.cloned.1.call-update) | async-done | bytes 1048592 | tf_op jit(solution)/shard_map/psum | solution.py:58
  190.0 1.4 negate_multiply_fusion.1
  191.5 1.0 copy-done.1
  192.5 2.0 fusion.10
  194.6 2.4 fusion.12
  197.3 1.7 convolution_bitcast_fusion.2
  199.0 153.8 %all-reduce.12.cloned.1.call-done = f32[8,256,128]{2,1,0:T(8,128)} async-done(((f32[8,256,128]{2,1,0:T(8,128)}), f32[8,256,128]{2,1,0:T(8,128)}) %all-reduce.12.cloned.1.call-update) | async-done | bytes 1048592 | tf_op jit(solution)/shard_map/psum | solution.py:60
  352.8 2.3 negate_multiply_fusion
  355.1 107.2 %all-gather.3.cloned.1.call-done = f32[8192,256]{1,0:T(8,128)} async-done(((f32[256,256]{1,0:T(8,128)}), f32[8192,256]{1,0:T(8,128)}) %all-gather.3.cloned.1.call-update) | async-done | bytes 8388624 | tf_op jit(solution)/shard_map/all_gather | solution.py:66
  462.4 4.7 reduce_sum.9
  467.1 2.4 fusion.11
  469.5 108.3 %all-reduce.10.cloned.1.call-done = f32[256,256]{1,0:T(8,128)} async-done(((f32[256,256]{1,0:T(8,128)}), f32[256,256]{1,0:T(8,128)}) %all-reduce.10.cloned.1.call-update) | async-done | bytes 262160 | tf_op jit(solution)/shard_map/psum | solution.py:67
  577.8 1.0 sub.15
  578.8 1.1 fusion.14
  580.0 157.6 %all-reduce.14.cloned.1.call-done = (f32[256,256]{1,0:T(8,128)}, f32[256,256]{1,0:T(8,128)}) async-done(((f32[256,256]{1,0:T(8,128)}, f32[256,256]{1,0:T(8,128)}), (f32[256,256]{1,0:T(8,128)}, f32[256,256]{1,0:T(8,128)})) %all-reduce.14.cloned.1.call-update) | async-done | bytes 524304 | tf_op jit(solution)/shard_map/psum | solution.py:74
  737.6 35.1 %all_gather.19 = f32[256,256]{1,0:T(8,128)S(1)} all-gather(f32[8,256]{1,0:T(8,128)S(1)} %copy-done.7), channel_id=1, replica_groups=mesh['prow'=32,'pcol'=16] {'prow'}, dimensions={0}, use_global_device_ids=true | all-gather | bytes 270336 | tf_op jit(solution)/shard_map/all_gather | solution.py:51
  772.8 1.4 dynamic-slice_bitcast_fusion.1
  774.1 1.4 dynamic-slice_bitcast_fusion
  775.5 80.7 %all-reduce.16.cloned.1.call-done = (f32[256,256]{1,0:T(8,128)}, f32[256,256]{1,0:T(8,128)}) async-done(((f32[256,256]{1,0:T(8,128)}, f32[256,256]{1,0:T(8,128)}), (f32[256,256]{1,0:T(8,128)}, f32[256,256]{1,0:T(8,128)})) %all-reduce.16.cloned.1.call-update) | async-done | bytes 524304 | tf_op jit(solution)/shard_map/psum | solution.py:75
  857.2 2.1 convolution_subtract_fusion
  (42 shorter events, 3.1 us)
Async XLA Ops:
  7.2 23.8 %copy-start = (f32[4,1,128,8,1,128]{5,4,3,2,1,0:T(1,128)S(1)}, f32[4,1,128,8,1,128]{5,4,3,2,1,0:T(1,128)}, u32[]{:S(2)}) copy-start(f32[4,1,128,8,1,128]{5,4,3,2,1,0:T(1,128)} %param.8) | copy-start | bytes 6291460
  7.2 182.8 %all-reduce.8.cloned.1.call-start = ((), (), s32[]{:S(2)}) async-start(), calls=%async_computation | async-start | bytes 2097152 | tf_op jit(solution)/shard_map/psum | solution.py:58
  31.0 3.3 copy-start.9
  31.0 3.8 copy-start.8
  34.2 318.6 %all-reduce.12.cloned.1.call-start = ((), (), s32[]{:S(2)}) async-start(), calls=%async_computation.2 | async-start | bytes 2097152 | tf_op jit(solution)/shard_map/psum | solution.py:60
  52.1 140.4 %copy-start.7 = (f32[8,256]{1,0:T(8,128)S(1)}, f32[8,256]{1,0:T(8,128)}, u32[]{:S(2)}) copy-start(f32[8,256]{1,0:T(8,128)} %param.11) | copy-start | bytes 24580
  190.0 2.5 copy-start.2
  191.5 1.1 copy-start.1
  194.6 267.8 %all-gather.3.cloned.1.call-start = ((), (), s32[]{:S(2)}) async-start(), calls=%async_computation.3 | async-start | bytes 8650752 | tf_op jit(solution)/shard_map/all_gather | solution.py:66
  197.0 380.7 %all-reduce.10.cloned.1.call-start = ((), (), s32[]{:S(2)}) async-start(), calls=%async_computation.1 | async-start | bytes 524288 | tf_op jit(solution)/shard_map/psum | solution.py:67
  462.4 115.4 %copy-start.5 = (f32[256,256]{1,0:T(8,128)S(1)}, f32[256,256]{1,0:T(8,128)}, u32[]{:S(2)}) copy-start(f32[256,256]{1,0:T(8,128)} %param.12) | copy-start | bytes 786436
  467.1 270.6 %all-reduce.14.cloned.1.call-start = ((), (), s32[]{:S(2)}) async-start(), calls=%async_computation.4 | async-start | bytes 1048576 | tf_op jit(solution)/shard_map/psum | solution.py:74
  469.5 387.7 %copy-start.6 = (f32[256,256]{1,0:T(8,128)S(1)}, f32[256,256]{1,0:T(8,128)}, u32[]{:S(2)}) copy-start(f32[256,256]{1,0:T(8,128)} %param.13) | copy-start | bytes 786436
  578.8 280.5 %copy-start.4 = (f32[256,256]{1,0:T(8,128)}, f32[256,256]{1,0:T(8,128)S(1)}, u32[]{:S(2)}) copy-start(f32[256,256]{1,0:T(8,128)S(1)} %sub.15) | copy-start | bytes 786436
  579.9 276.2 %all-reduce.16.cloned.1.call-start = ((), (), s32[]{:S(2)}) async-start(), calls=%async_computation.5 | async-start | bytes 1048576 | tf_op jit(solution)/shard_map/psum | solution.py:75
  857.1 2.2 copy-start.3
Sparse Core Ops, SparseCore 0:
  34.3 155.6 all-reduce.7
  194.7 158.0 all-reduce.11
  356.6 105.7 all-gather.2
  467.2 110.5 all-reduce.9
  582.0 155.5 all-reduce.13
  739.9 116.2 all-reduce.15
